TPU v7x, 32 devices: a whole 2x2x4 slice. The times are simulated.
32 devices in a mesh: seq: 32 (over z, y, x, core), head: 1.
Axes of the slice: x: 2, y: 2, z: 4, core: 2. Of those that a mesh axis runs over, the one named last changes fastest.
Arguments:
- tokens: bfloat16 [131072, 256], P('seq'), may hold values from -6 to 6
- fine_gain: float32 [256], replicated, may hold values from 0.1 to 1.9
- fine_gate: bfloat16 [256, 512], P(None, 'head'), may hold values from -0.375 to 0.375
- fine_value: bfloat16 [256, 512], P(None, 'head'), may hold values from -0.375 to 0.375
- fine_scans: bfloat16 [256, 512], replicated, may hold values from -0.375 to 0.375
- fine_steps: bfloat16 [256, 8], P(None, 'head'), may hold values from -0.375 to 0.375
- fine_kernel: float32 [4, 512], P(None, 'head'), may hold values from -3 to 3
- fine_taps: float32 [4, 512], replicated, may hold values from -3 to 3
- fine_bias: float32 [8], P('head'), may hold values from -3 to 1
- fine_decay: float32 [8], P('head'), may hold values from 7.6293945e-06 to 0.2
- fine_norm: float32 [512], P('head'), may hold values from 0.1 to 1.9
- fine_output: bfloat16 [512, 256], P('head'), may hold values from -0.25 to 0.25
- merge_weight: bfloat16 [1024, 1024], replicated, may hold values from -0.1875 to 0.1875
- coarse_gain: float32 [1024], replicated, may hold values from 0.1 to 1.9
- coarse_gate: bfloat16 [1024, 2048], P(None, 'head'), may hold values from -0.1875 to 0.1875
- coarse_value: bfloat16 [1024, 2048], P(None, 'head'), may hold values from -0.1875 to 0.1875
- coarse_scans: bfloat16 [1024, 512], replicated, may hold values from -0.1875 to 0.1875
- coarse_steps: bfloat16 [1024, 32], P(None, 'head'), may hold values from -0.1875 to 0.1875
- coarse_kernel: float32 [4, 2048], P(None, 'head'), may hold values from -3 to 3
- coarse_taps: float32 [4, 512], replicated, may hold values from -3 to 3
- coarse_bias: float32 [32], P('head'), may hold values from -3 to 1
- coarse_decay: float32 [32], P('head'), may hold values from 3.0517578e-05 to 0.2
- coarse_norm: float32 [2048], P('head'), may hold values from 0.1 to 1.9
- coarse_output: bfloat16 [2048, 1024], P('head'), may hold values from -0.125 to 0.125
Outputs:
- scene_tokens: bfloat16 [32768, 1024], P('seq', 'head')
All inputs are finite; a program needn't handle non-finite values.
Results may differ from a plain program's by a relative error of at most 0.02.
Values may be sent and summed in bfloat16 or wider, within the bound.
A program may use at most 192 MiB of HBM per device.

v0:
```python
import jax
import jax.numpy as jnp
from jax import lax
from jax.sharding import PartitionSpec as P

INNER = 512
HEAD_DIM = 64
STATE = 256
COARSE_INNER = 2048
KERNEL = 4
BLOCK = 256
ROW_PATCHES = 64


EPSILON = 1e-05


def carried_in(x, axis, combine, identity):
    count, index = (lax.axis_size(axis), lax.axis_index(axis))
    everything = jax.tree.map(
        lambda part, kind: lax.all_gather(part.astype(kind), axis), x, (jnp.bfloat16, jnp.bfloat16)
    )
    start = jax.tree.map(
        lambda part, zero: jnp.broadcast_to(jnp.asarray(zero, part.dtype), part.shape), x, identity
    )

    def lap(k, before):
        reached = k < index
        new = combine(
            before, jax.tree.map(lambda part, own: part[k].astype(own.dtype), everything, x)
        )
        return jax.tree.map(lambda a, b: jnp.where(reached, a, b), new, before)

    return lax.fori_loop(0, count, lap, start)


def passed_along(block, axis, distance):
    devices = range(lax.axis_size(axis))
    route = [(i - distance, i) for i in devices if i - distance in devices]
    return lax.ppermute(block, axis, route)


def rms_rows(values, gain_vec):
    return (
        values * lax.rsqrt(jnp.mean(values * values, axis=-1, keepdims=True) + EPSILON) * gain_vec
    )


def chain_combine(earlier, later):
    return (earlier[0] * later[0], later[0][:, None, None] * earlier[1] + later[1])


def local_scan(conv_values, step_sizes, log_decay, input_map, output_map, coarse):
    length = conv_values.shape[0]
    heads_here = step_sizes.shape[1]
    blocks = length // BLOCK
    vals = conv_values.reshape(blocks, BLOCK, heads_here, HEAD_DIM)
    dts = step_sizes.reshape(blocks, BLOCK, heads_here)
    logs_blk = log_decay.reshape(blocks, BLOCK, heads_here)
    b_blk = input_map.reshape(blocks, BLOCK, STATE)
    c_blk = output_map.reshape(blocks, BLOCK, STATE)
    cumul = jnp.cumsum(logs_blk, axis=1)
    scores = jnp.einsum("ctn,csn->cts", c_blk, b_blk, preferred_element_type=jnp.float32)
    by_head = cumul.transpose(0, 2, 1)
    spread = by_head[:, :, :, None] - by_head[:, :, None, :]
    lower = jnp.tril(jnp.ones((BLOCK, BLOCK), dtype=bool))
    decays = jnp.exp(jnp.where(lower[None, None], spread, -jnp.inf))
    weights = (scores[:, None] * decays * dts.transpose(0, 2, 1)[:, :, None, :]).astype(
        jnp.bfloat16
    )
    intra = jnp.einsum("chts,cshp->cthp", weights, vals, preferred_element_type=jnp.float32)
    tail_w = jnp.exp(cumul[:, -1:, :] - cumul) * dts
    scaled = (vals.astype(jnp.float32) * tail_w[..., None]).astype(jnp.bfloat16)
    local = jnp.einsum("cshp,csn->chpn", scaled, b_blk, preferred_element_type=jnp.float32)
    totals = cumul[:, -1, :]

    def advance(carried, element):
        total_log, piece = element
        return (jnp.exp(total_log)[:, None, None] * carried + piece, carried)

    device_state, prefix = lax.scan(
        advance, jnp.zeros((heads_here, HEAD_DIM, STATE), jnp.float32), (totals, local)
    )
    device_decay = jnp.exp(jnp.sum(totals, axis=0))
    identity = (
        jnp.ones((heads_here,), jnp.float32),
        jnp.zeros((heads_here, HEAD_DIM, STATE), jnp.float32),
    )
    if coarse:
        _, incoming = carried_in((device_decay, device_state), "seq", chain_combine, identity)
    else:
        _, incoming = carried_in((device_decay, device_state), "seq", chain_combine, identity)
    before = jnp.cumsum(totals, axis=0) - totals
    start_state = prefix + jnp.exp(before)[:, :, None, None] * incoming[None]
    inter = jnp.einsum(
        "ctn,chpn->cthp", c_blk.astype(jnp.float32), start_state, precision=lax.Precision.HIGHEST
    )
    inter = inter * jnp.exp(cumul)[..., None]
    return (intra + inter).reshape(length, heads_here * HEAD_DIM)


def mamba_local(
    stream,
    gain_vec,
    gate_weight,
    value_weight,
    scan_weight,
    step_weight,
    kernel_value,
    kernel_scan,
    step_bias,
    decay_rate,
    norm_gain,
    out_weight,
    inner_total,
    coarse,
):
    normed = rms_rows(stream.astype(jnp.float32), gain_vec).astype(jnp.bfloat16)
    gate_rows = jnp.dot(normed, gate_weight, preferred_element_type=jnp.float32).astype(
        jnp.bfloat16
    )
    value_rows = jnp.dot(normed, value_weight, preferred_element_type=jnp.float32).astype(
        jnp.bfloat16
    )
    scan_rows = jnp.dot(normed, scan_weight, preferred_element_type=jnp.float32).astype(
        jnp.bfloat16
    )
    step_raw = jnp.dot(normed, step_weight, preferred_element_type=jnp.float32)
    joined = jnp.concatenate([value_rows, scan_rows], 1)
    length = joined.shape[0]
    tail_rows = joined[length - (KERNEL - 1) :]
    if coarse:
        rim_rows = passed_along(tail_rows, "seq", 1)
    else:
        rim_rows = passed_along(tail_rows, "seq", 1)
    kernels = jnp.concatenate([kernel_value, kernel_scan], 1)
    padded = jnp.concatenate([rim_rows, joined], 0).astype(jnp.float32)
    summed = jnp.zeros(joined.shape, jnp.float32)
    for offset in range(KERNEL):
        summed = summed + padded[offset : offset + length] * kernels[offset]
    convolved = jax.nn.silu(summed).astype(jnp.bfloat16)
    width_here = value_rows.shape[1]
    conv_values = convolved[:, :width_here]
    input_map = convolved[:, width_here : width_here + STATE]
    output_map = convolved[:, width_here + STATE :]
    step_sizes = jax.nn.softplus(step_raw + step_bias)
    log_decay = -step_sizes * decay_rate
    mixed_rows = local_scan(conv_values, step_sizes, log_decay, input_map, output_map, coarse)
    gated_rows = mixed_rows * jax.nn.silu(gate_rows.astype(jnp.float32))
    squares = jnp.sum(gated_rows * gated_rows, axis=1)
    if coarse:
        square_sum = lax.psum(squares, "head")
    else:
        square_sum = lax.psum(squares, "head")
    scaled = gated_rows * lax.rsqrt(square_sum / inner_total + EPSILON)[:, None] * norm_gain
    normed_out = scaled.astype(jnp.bfloat16)
    return jnp.dot(normed_out, out_weight, preferred_element_type=jnp.float32)


def merge_tiles(rows):
    count, width_here = rows.shape
    grid = rows.reshape(count // (2 * ROW_PATCHES), 2, ROW_PATCHES // 2, 2, width_here)
    return grid.transpose(0, 2, 1, 3, 4).reshape(count // 4, 4 * width_here)


def shards(
    tokens,
    fine_gain,
    fine_gate,
    fine_value,
    fine_scans,
    fine_steps,
    fine_kernel,
    fine_taps,
    fine_bias,
    fine_decay,
    fine_norm,
    fine_output,
    merge_weight,
    coarse_gain,
    coarse_gate,
    coarse_value,
    coarse_scans,
    coarse_steps,
    coarse_kernel,
    coarse_taps,
    coarse_bias,
    coarse_decay,
    coarse_norm,
    coarse_output,
):
    position = lax.axis_index("head")
    groups = lax.axis_size("head")
    branch = mamba_local(
        tokens,
        fine_gain,
        fine_gate,
        fine_value,
        fine_scans,
        fine_steps,
        fine_kernel,
        fine_taps,
        fine_bias,
        fine_decay,
        fine_norm,
        fine_output,
        INNER,
        False,
    )
    full_sum = lax.psum(branch.astype(jnp.bfloat16), "head").astype(jnp.float32)
    hidden = (tokens.astype(jnp.float32) + full_sum).astype(jnp.bfloat16)
    tiles = merge_tiles(hidden)
    merge_cols = merge_weight.shape[1] // groups
    weight_cols = lax.dynamic_slice_in_dim(merge_weight, position * merge_cols, merge_cols, 1)
    merged_share = jnp.dot(tiles, weight_cols, preferred_element_type=jnp.float32).astype(
        jnp.bfloat16
    )
    merged = lax.all_gather(merged_share, "head", axis=1, tiled=True)
    branch_two = mamba_local(
        merged,
        coarse_gain,
        coarse_gate,
        coarse_value,
        coarse_scans,
        coarse_steps,
        coarse_kernel,
        coarse_taps,
        coarse_bias,
        coarse_decay,
        coarse_norm,
        coarse_output,
        COARSE_INNER,
        True,
    )
    final_sum = lax.psum_scatter(
        branch_two.astype(jnp.bfloat16), "head", scatter_dimension=1, tiled=True
    ).astype(jnp.float32)
    out_cols = merged.shape[1] // groups
    merged_share_cols = lax.dynamic_slice_in_dim(merged, position * out_cols, out_cols, 1)
    return (merged_share_cols.astype(jnp.float32) + final_sum).astype(jnp.bfloat16)


def solution(mesh):
    return jax.shard_map(
        shards,
        mesh=mesh,
        in_specs=(
            P("seq", None),
            P(),
            P(None, "head"),
            P(None, "head"),
            P(),
            P(None, "head"),
            P(None, "head"),
            P(),
            P("head"),
            P("head"),
            P("head"),
            P("head", None),
            P(),
            P(),
            P(None, "head"),
            P(None, "head"),
            P(),
            P(None, "head"),
            P(None, "head"),
            P(),
            P("head"),
            P("head"),
            P("head"),
            P("head", None),
        ),
        out_specs=P("seq", "head"),
        check_vma=False,
    )
```

profile of v0, /device:TPU:0, one launch (start us, length us, event | category | flops | bytes accessed | tf_op | source)
XLA Modules:
  0.0 710.1 jit_solution(668432643910653431)
XLA Ops:
  6.5 2.4 fusion.42
  9.0 3.2 convolution_convert_fusion.1
  16.3 3.5 collective-permute-start
  20.6 9.0 %reduce-window.14 = f32[16,8,2,128]{3,1,2,0:T(8,128)S(1)} reduce-window(f32[16,8,2,128]{3,1,2,0:T(8,128)S(1)} %bitcast.200, f32[]{:T(128)} %constant.118.clone.1), window={size=1x1x1x128 pad=0_0x0_0x0_0x127_0}, to_apply=%region_1.2 | reduce-window | flops 4161536 | bytes 262148 | tf_op jit(solution)/shard_map/reduce-window
  30.7 13.7 %maximum_convert_fusion = f32[4099,1024]{0,1:T(8,128)} fusion(bf16[4096,512]{0,1:T(8,128)(2,1)} %copy-done.5, bf16[4096,512]{0,1:T(8,128)(2,1)} %copy-done.6, bf16[3,1024]{0,1:T(8,128)(2,1)} %collective-permute-done), kind=kLoop, calls=%fused_computation.52 | loop fusion | flops 25184256 | bytes 25184256 | tf_op jit(solution)/shard_map/convert_element_type | solution.py:137
  44.4 33.4 %multiply_convert_fusion.4 = bf16[4096,1024]{0,1:T(8,128)(2,1)S(1)} fusion(f32[4099,1024]{0,1:T(8,128)} %maximum_convert_fusion, f32[1024]{0:T(1024)S(1)} %bitcast.203, f32[1024]{0:T(1024)S(1)} %bitcast.204, f32[1024]{0:T(1024)S(1)} %bitcast.205, f32[1024]{0:T(1024)S(1)} %bitcast.202), kind=kLoop, calls=%fused_computation.37 | loop fusion | flops 50331648 | bytes 75513856 | tf_op jit(solution)/shard_map/convert_element_type | solution.py:141
  86.1 5.3 fusion.49
  91.4 32.8 %while.54 = (s32[]{:T(128)}, f32[8,64,256]{2,1,0:T(8,128)S(1)}, f32[16,8,64,256]{3,2,1,0:T(8,128)}, f32[16,8]{1,0:T(8,128)S(1)}, f32[16,8,64,256]{3,2,1,0:T(8,128)}, /*index=5*/s32[]{:T(128)}, s32[]{:T(128)}) while((s32[]{:T(128)}, f32[8,64,256]{2,1,0:T(8,128)S(1)}, f32[16,8,64,256]{3,2,1,0:T(8,128)}, f32[16,8]{1,0:T(8,128)S(1)}, ...), condition=%wide.region_4.5_spmd.clone, body=%wide.region_3.4_spmd.clone.sunk | while | flops 524291 | bytes 2622144 | solution.py:81
  125.4 41.6 %all-reduce = bf16[256]{0:T(256)(128)(2,1)S(1)} all-reduce(bf16[256]{0:T(256)(128)(2,1)S(1)} %dynamic-update-slice), channel_id=2, replica_groups=mesh['seq'=32,'head'=1] {'seq'}, use_global_device_ids=true, to_apply=%add | all-reduce | flops 256 | bytes 1024
  168.8 3.6 copy.162
  174.7 12.2 %fusion.6 = f32[16,8,64,256]{3,2,1,0:T(8,128)} fusion(f32[16,8,256]{2,1,0:T(8,128)S(1)} %bitcast.196, f32[16,8,256]{2,1,0:T(8,128)S(1)} %add_bitcast_fusion.2, f32[16,256,256]{2,1,0:T(8,128)S(1)} %fusion.69, pred[256,256]{1,0:T(8,128)(4,1)S(1)} %iota_compare_fusion, bf16[16,256,8,64]{1,0,3,2:T(8,128)(2,1)S(1)} %bitcast.176), kind=kOutput, calls=%fused_computation.18 | convolution fusion | flops 1115684864 | bytes 17104896 | tf_op jit(solution)/shard_map/chts,cshp->cthp/dot_general | solution.py:71
  186.8 17.8 %all-gather.7.cloned.1.call-done = bf16[256,64,256]{2,1,0:T(8,128)(2,1)} async-done(((bf16[8,64,256]{2,1,0:T(8,128)(2,1)}), bf16[256,64,256]{2,1,0:T(8,128)(2,1)}) %all-gather.7.cloned.1.call-update) | async-done | bytes 8388624 | tf_op jit(solution)/shard_map/all_gather | solution.py:21
  204.7 36.6 %while.55 = (s32[]{:T(128)}, f32[8,64,256]{2,1,0:T(8,128)S(1)}, s32[]{:T(128)}, bf16[32,8]{1,0:T(8,128)(2,1)S(1)}, bf16[32,8,64,256]{3,2,1,0:T(8,128)(2,1)}, /*index=5*/s32[]{:T(128)}, s32[]{:T(128)}) while((s32[]{:T(128)}, f32[8,64,256]{2,1,0:T(8,128)S(1)}, s32[]{:T(128)}, bf16[32,8]{1,0:T(8,128)(2,1)S(1)}, ...), condition=%wide.region_8.9_spmd.clone, body=%wide.region_7.8_spmd.clone.sunk | while | flops 655372 | bytes 1310905 | solution.py:34
  241.2 12.6 %bitcast_add_fusion.3 = f32[16,256,8,64]{1,3,2,0:T(8,128)S(1)} fusion(f32[16,8,64,256]{3,2,1,0:T(8,128)} %fusion.6, f32[16,256,8]{1,2,0:T(8,128)S(1)} %get-tuple-element.393, f32[16,8,64,256]{3,2,1,0:T(8,128)} %get-tuple-element.249, f32[8,64,256]{2,1,0:T(8,128)S(1)} %get-tuple-element.251, f32[16,8]{1,0:T(8,128)S(1)} %subtract_exponential_fusion, ...), kind=kOutput, calls=%fused_computation.62 | convolution fusion | flops 6450839552 | bytes 27918848 | tf_op jit(solution)/shard_map/ctn,chpn->cthp/dot_general | solution.py:95
  253.8 4.8 copy.121
  258.6 8.4 %copy.164 = f32[64,8,16,256]{3,1,2,0:T(8,128)S(1)} copy(f32[64,8,16,256]{3,2,1,0:T(8,128)S(1)} %bitcast.178) | data formatting | bytes 16777216
  267.1 3.4 multiply_reduce_fusion.1
  270.5 4.0 fusion.41
  274.5 4.1 reshape.247
  278.6 4.7 copy.199
  283.2 4.4 reshape.248
  287.7 4.0 fusion.45
  293.1 2.3 reduce-window.16
  297.2 7.7 %convolution_convert_fusion.4 = bf16[1024,2048]{1,0:T(8,128)(2,1)S(1)} fusion(bf16[1024,2048]{1,0:T(8,128)(2,1)} %param.47, bf16[1024,1024]{0,1:T(8,128)(2,1)} %copy-done.40, f32[1024]{0:T(1024)S(1)} %copy-done.34, f32[1024]{0:T(1024)S(1)} %add_rsqrt_fusion.3), kind=kOutput, calls=%fused_computation.110 | convolution fusion | flops 4301258752 | bytes 10493952 | tf_op jit(solution)/shard_map/dot_general | solution.py:122
  309.9 3.5 maximum_convert_fusion.1
  313.5 7.6 %multiply_convert_fusion.5 = bf16[1024,2560]{1,0:T(8,128)(2,1)} fusion(f32[1027,2560]{1,0:T(8,128)S(1)} %maximum_convert_fusion.1, f32[2560]{0:T(1024)S(1)} %copy-done.17, f32[2560]{0:T(1024)S(1)} %copy-done.18, f32[2560]{0:T(1024)S(1)} %copy-done.19, f32[2560]{0:T(1024)S(1)} %get-tuple-element.349), kind=kLoop, calls=%fused_computation.51 | loop fusion | flops 31457280 | bytes 47226880 | tf_op jit(solution)/shard_map/convert_element_type | solution.py:141
  321.1 4.8 slice.144
  327.2 6.4 copy.124
  333.6 7.8 %reshape.249 = bf16[4,256,32,64]{1,0,3,2:T(4,128)(2,1)} reshape(bf16[1024,2048]{0,1:T(8,128)(2,1)} %copy.124) | data formatting | bytes 8388608 | tf_op jit(solution)/shard_map/reshape | solution.py:57
  341.4 4.3 multiply_convert_fusion.7
  345.7 4.5 fusion.51
  350.2 14.2 %while.56 = (s32[]{:T(128)}, f32[32,64,256]{2,1,0:T(8,128)S(1)}, f32[4,32,64,256]{3,2,1,0:T(8,128)}, f32[4,32]{1,0:T(4,128)S(1)}, f32[4,32,64,256]{3,2,1,0:T(8,128)}, /*index=5*/s32[]{:T(128)}, s32[]{:T(128)}) while((s32[]{:T(128)}, f32[32,64,256]{2,1,0:T(8,128)S(1)}, f32[4,32,64,256]{3,2,1,0:T(8,128)}, f32[4,32]{1,0:T(4,128)S(1)}, ...), condition=%wide.region_14.15_spmd.clone, body=%wide.region_13.14_spmd.clone.sunk | while | flops 2097155 | bytes 10486752 | solution.py:81
  366.0 45.3 %all-reduce.1 = bf16[1024]{0:T(1024)(128)(2,1)S(1)} all-reduce(bf16[1024]{0:T(1024)(128)(2,1)S(1)} %dynamic-update-slice.1), channel_id=4, replica_groups=mesh['seq'=32,'head'=1] {'seq'}, use_global_device_ids=true, to_apply=%add.1 | all-reduce | flops 1024 | bytes 4096
  411.8 13.3 %fusion.7 = f32[4,32,64,256]{3,2,1,0:T(8,128)} fusion(f32[4,32,256]{2,1,0:T(8,128)S(1)} %copy.130, f32[4,32,256]{2,1,0:T(8,128)} %get-tuple-element.402, f32[4,256,256]{2,1,0:T(8,128)S(1)} %fusion.95, pred[256,256]{1,0:T(8,128)(4,1)} %copy-done.16, bf16[4,256,32,64]{1,0,3,2:T(4,128)(2,1)} %reshape.249), kind=kOutput, calls=%fused_computation.19 | convolution fusion | flops 1115684864 | bytes 13959168 | tf_op jit(solution)/shard_map/chts,cshp->cthp/dot_general | solution.py:71
  425.1 138.2 %all-gather.9.cloned.1.call-done = bf16[1024,64,256]{2,1,0:T(8,128)(2,1)} async-done(((bf16[32,64,256]{2,1,0:T(8,128)(2,1)}), bf16[1024,64,256]{2,1,0:T(8,128)(2,1)}) %all-gather.9.cloned.1.call-update) | async-done | bytes 33554448 | tf_op jit(solution)/shard_map/all_gather | solution.py:21
  563.3 72.5 %while.57 = (s32[]{:T(128)}, f32[32,64,256]{2,1,0:T(8,128)S(1)}, s32[]{:T(128)}, bf16[32,32]{1,0:T(8,128)(2,1)S(1)}, bf16[32,32,64,256]{3,2,1,0:T(8,128)(2,1)}, /*index=5*/s32[]{:T(128)}, s32[]{:T(128)}) while((s32[]{:T(128)}, f32[32,64,256]{2,1,0:T(8,128)S(1)}, s32[]{:T(128)}, bf16[32,32]{1,0:T(8,128)(2,1)S(1)}, ...), condition=%wide.region_18.19_spmd.clone, body=%wide.region_17.18_spmd.clone.sunk | while | flops 2621476 | bytes 5243305 | solution.py:34
  565.5 2.2 fusion.119
  567.8 2.2 fusion.119
  574.6 2.2 fusion.119
  576.9 2.2 fusion.119
  583.7 2.2 fusion.119
  586.0 2.2 fusion.119
  635.8 13.9 %bitcast_add_fusion.2 = f32[4,256,32,64]{1,3,2,0:T(8,128)} fusion(f32[4,32,64,256]{3,2,1,0:T(8,128)} %fusion.7, f32[4,256,32]{1,2,0:T(8,128)S(1)} %get-tuple-element.400, bf16[4,256,256,1]{2,1,3,0:T(8,128)(2,1)S(1)} %bitcast.188, f32[4,32,64,256]{3,2,1,0:T(8,128)} %get-tuple-element.252, f32[32,64,256]{2,1,0:T(8,128)S(1)} %get-tuple-element.254, ...), kind=kOutput, calls=%fused_computation.61 | convolution fusion | flops 6450839552 | bytes 27918848 | tf_op jit(solution)/shard_map/ctn,chpn->cthp/dot_general | solution.py:95
  649.7 16.2 %copy.153 = f32[4,256,32,64]{3,2,1,0:T(8,128)} copy(f32[4,256,32,64]{1,3,2,0:T(8,128)} %bitcast_add_fusion.2) | data formatting | bytes 16777216 | tf_op jit(solution)/shard_map/reshape | solution.py:99
  665.9 15.1 %reshape.277 = f32[1024,2048]{1,0:T(8,128)} reshape(f32[4,256,32,64]{3,2,1,0:T(8,128)} %copy.153) | data formatting | bytes 16777216 | tf_op jit(solution)/shard_map/reshape | solution.py:99
  681.1 11.8 %multiply_reduce_fusion = (f32[1024]{0:T(1024)S(1)}, f32[1024,2048]{1,0:T(8,128)S(1)}) fusion(f32[1024,2048]{1,0:T(8,128)} %reshape.277, bf16[1024,2048]{1,0:T(8,128)(2,1)} %param.46, bf16[1024,1024]{0,1:T(8,128)(2,1)} %copy-done.40, f32[1024]{0:T(1024)S(1)} %copy-done.35, f32[1024]{0:T(1024)S(1)} %copy-done.26), kind=kOutput, calls=%fused_computation.64 | convolution fusion | flops 4318034944 | bytes 23080960 | tf_op jit(solution)/shard_map/dot_general | solution.py:119
  692.9 6.1 fusion.48
  699.0 3.9 copy.138
  (342 shorter events, 170.6 us)
Async XLA Ops:
  6.5 281.1 %copy-start = (bf16[1024,1024]{1,0:T(8,128)(2,1)S(1)}, bf16[1024,1024]{1,0:T(8,128)(2,1)}, u32[]{:S(2)}) copy-start(bf16[1024,1024]{1,0:T(8,128)(2,1)} %param.44) | copy-start | bytes 6291460
  6.5 198.1 %all-gather.7.cloned.1.call-start = ((), (), s32[]{:S(2)}) async-start(), calls=%async_computation | async-start | bytes 8650752 | tf_op jit(solution)/shard_map/all_gather | solution.py:21
  8.9 3.2 copy-start.3
  8.9 3.2 copy-start.15
  8.9 3.2 copy-start.20
  12.2 2.0 copy-start.5
  14.2 2.1 copy-start.6
  14.2 5.5 copy-start.33
  14.2 5.6 copy-start.36
  14.2 5.6 copy-start.37
  16.3 14.2 %copy-start.22 = (f32[4,512]{1,0:T(4,128)S(1)}, f32[4,512]{1,0:T(4,128)}, u32[]{:S(2)}) copy-start(f32[4,512]{1,0:T(4,128)} %param.38) | copy-start | bytes 24580
  16.3 14.3 %copy-start.23 = (f32[4,512]{1,0:T(4,128)S(1)}, f32[4,512]{1,0:T(4,128)}, u32[]{:S(2)}) copy-start(f32[4,512]{1,0:T(4,128)} %param.39) | copy-start | bytes 24580
  16.3 14.4 %collective-permute-start = (bf16[3,1024]{0,1:T(8,128)(2,1)}, bf16[3,1024]{0,1:T(8,128)(2,1)}, u32[]{:S(2)}, u32[]{:S(2)}) collective-permute-start(bf16[3,1024]{0,1:T(8,128)(2,1)} %pad_maximum_fusion), channel_id=1, source_target_pairs={{0,1},{1,2},{2,3},{3,4},{4,5},{5,6},{6,7},{7,8},{8,9},{9,10},{10,1... | collective-permute-start | bytes 18440 | tf_op jit(solution)/shard_map/ppermute | solution.py:40
  77.8 3.9 copy-start.9
  81.7 1.4 copy-start.11
  81.7 2.9 slice-start
  86.1 5.3 copy-start.7
  91.4 76.6 %copy-start.24 = (f32[4,512]{1,0:T(4,128)S(1)}, f32[4,512]{1,0:T(4,128)}, u32[]{:S(2)}) copy-start(f32[4,512]{1,0:T(4,128)} %param.51) | copy-start | bytes 24580
  125.0 438.3 %all-gather.9.cloned.1.call-start = ((), (), s32[]{:S(2)}) async-start(), calls=%async_computation.1 | async-start | bytes 34603008 | tf_op jit(solution)/shard_map/all_gather | solution.py:21
  167.0 5.4 copy-start.10
  167.1 5.4 copy-start.12
  168.0 5.2 copy-start.16
  172.5 2.2 copy-start.8
  258.6 8.4 %copy-start.4 = (bf16[4096,256]{1,0:T(8,128)(2,1)S(1)}, bf16[4096,256]{1,0:T(8,128)(2,1)}, u32[]{:S(2)}) copy-start(bf16[4096,256]{1,0:T(8,128)(2,1)} %param.32) | copy-start | bytes 6291460
  258.6 8.4 %copy-start.30 = (bf16[256,512]{1,0:T(8,128)(2,1)S(1)}, bf16[256,512]{1,0:T(8,128)(2,1)}, u32[]{:S(2)}) copy-start(bf16[256,512]{1,0:T(8,128)(2,1)} %param.34) | copy-start | bytes 786436
  267.0 3.5 copy-start.14
  267.0 3.5 copy-start.21
  287.7 4.1 copy-start.31
  287.7 4.1 copy-start.34
  287.7 4.1 copy-start.38
  287.7 4.1 copy-start.39
  291.8 1.3 copy-start.40
  291.8 13.1 %copy-start.25 = (f32[1024]{0:T(1024)}, f32[1024]{0:T(1024)S(1)}, u32[]{:S(2)}) copy-start(f32[1024]{0:T(1024)S(1)} %add_rsqrt_fusion.3) | copy-start | bytes 12292
  297.2 7.7 %copy-start.29 = (bf16[1024,512]{1,0:T(8,128)(2,1)S(1)}, bf16[1024,512]{1,0:T(8,128)(2,1)}, u32[]{:S(2)}) copy-start(bf16[1024,512]{1,0:T(8,128)(2,1)} %param.48) | copy-start | bytes 3145732
  297.2 7.7 %copy-start.41 = (bf16[1024,1024]{0,1:T(8,128)(2,1)S(1)}, bf16[1024,1024]{0,1:T(8,128)(2,1)}, u32[]{:S(2)}) copy-start(bf16[1024,1024]{0,1:T(8,128)(2,1)} %copy-done.40) | copy-start | bytes 6291460
  304.9 1.9 copy-start.13
  306.9 3.0 collective-permute-start.1
  309.3 4.1 copy-start.17
  309.3 4.1 copy-start.18
  309.3 4.1 copy-start.19
  345.7 4.5 copy-start.2
  364.5 1.3 copy-start.27
  665.9 15.1 %copy-start.26 = (f32[1024]{0:T(1024)S(1)}, f32[1024]{0:T(1024)}, u32[]{:S(2)}) copy-start(f32[1024]{0:T(1024)} %copy-done.25) | copy-start | bytes 12292
  665.9 15.1 %copy-start.35 = (f32[1024]{0:T(1024)S(1)}, f32[1024]{0:T(1024)}, u32[]{:S(2)}) copy-start(f32[1024]{0:T(1024)} %param.45) | copy-start | bytes 12292
  681.0 11.8 %copy-start.28 = (bf16[2048,1024]{1,0:T(8,128)(2,1)S(1)}, bf16[2048,1024]{1,0:T(8,128)(2,1)}, u32[]{:S(2)}) copy-start(bf16[2048,1024]{1,0:T(8,128)(2,1)} %param.55) | copy-start | bytes 12582916
  681.0 11.8 %copy-start.32 = (f32[2048]{0:T(1024)S(1)}, f32[2048]{0:T(1024)}, u32[]{:S(2)}) copy-start(f32[2048]{0:T(1024)} %param.54) | copy-start | bytes 24580
  681.1 11.8 %copy-start.42 = (bf16[1024,1024]{0,1:T(8,128)(2,1)S(1)}, bf16[1024,1024]{0,1:T(8,128)(2,1)}, u32[]{:S(2)}) copy-start(bf16[1024,1024]{0,1:T(8,128)(2,1)} %copy-done.40) | copy-start | bytes 6291460
  692.9 10.1 %copy-start.1 = (bf16[1024,1024]{1,0:T(8,128)(2,1)S(1)}, bf16[1024,1024]{1,0:T(8,128)(2,1)}, u32[]{:S(2)}) copy-start(bf16[1024,1024]{1,0:T(8,128)(2,1)} %param.44) | copy-start | bytes 6291460
Sparse Core Ops, SparseCore 0:
  125.1 79.4 all-gather.6
  365.7 197.4 all-gather.8
where the time goes:
time: 718 us; the launch traced here: 710 us
  other arithmetic  235 us (33%)
  waiting for transfers between devices  157 us (22%)
  matrix products  108 us (15%)
  local copies, waits for them, and re-layouts  101 us (14%)
  blocking collectives  86.9 us (12%)
  between operations  14.6 us (2%)
    all_gather x2, waiting for transfers between devices, carried_in(): lax.all_gather(part.astype(kind), axis)  156 us
    select_n x64, other arithmetic, lap(): return jax.tree.map(lambda a, b: jnp.where(reached, a, b), new, before)  106 us
    unnamed x2, blocking collectives  86.9 us
    convert_element_type x2, other arithmetic, mamba_local(): convolved = jax.nn.silu(summed).astype(jnp.bfloat16)  41 us
    reshape x2, local copies, waits for them, and re-layouts, local_scan(): return (intra + inter).reshape(length, heads_here * HEAD_DIM)  31.3 us
    dot_general x2, matrix products, local_scan(): jnp.einsum('ctn,chpn->cthp', c_blk.astype(jnp.float32), start_state, prec...  26.5 us
    add x20, other arithmetic, advance(): return (jnp.exp(total_log)[:, None, None] * carried + piece, carried)  26.5 us
    dot_general x2, matrix products, local_scan(): jnp.einsum('chts,cshp->cthp', weights, vals, preferred_element_type=jnp.f...  25.5 us
  transfers between devices with their start and end apart: 4, of which 3 were waited for; matrix products, arithmetic and copies ran while one was open for 6% of the time, Pallas kernels for 0%

commit v1 on v0

v1 whole, which is shorter than its diff:
```python
import functools

import jax
import jax.numpy as jnp
from jax import lax
from jax.experimental import pallas as pl
from jax.experimental.pallas import tpu as pltpu
from jax.sharding import PartitionSpec as P

HEAD_DIM = 64
BLOCK = 256
ROW_PATCHES = 64
LANES = 128
RIM = 16
EPSILON = 1e-05
VMEM_LIMIT = 48 * 1024 * 1024
F32 = jnp.float32
BF16 = jnp.bfloat16


def whole(shape):
    return pl.BlockSpec(shape, lambda i: (0,) * len(shape), pipeline_mode=pl.Buffered(1))


def rows_of(width):
    return pl.BlockSpec((BLOCK, width), lambda i: (i, 0))


def params():
    return pltpu.CompilerParams(
        dimension_semantics=("arbitrary",), vmem_limit_bytes=VMEM_LIMIT
    )


def rms(values, gain):
    mean = jnp.mean(values * values, axis=-1, keepdims=True)
    return values * lax.rsqrt(mean + EPSILON) * gain


def silu(v):
    half = 0.5 * v
    return half + half * jnp.tanh(half)


def head_groups(heads):
    per = LANES // HEAD_DIM
    if heads % per:
        per = 1
    return per, heads // per


def over_lanes(columns, first, per):
    n = columns.shape[0]
    width = per * HEAD_DIM
    lane = lax.broadcasted_iota(jnp.int32, (n, width), 1)
    out = jnp.broadcast_to(columns[:, first : first + 1], (n, width))
    for k in range(1, per):
        out = jnp.where(lane >= k * HEAD_DIM, columns[:, first + k : first + k + 1], out)
    return out


def to_columns(by_head):
    heads = by_head.shape[0]
    if heads < LANES:
        by_head = jnp.concatenate([by_head, jnp.zeros((LANES - heads, BLOCK), F32)], 0)
    return by_head.T


def dot(a, b):
    return jnp.dot(a, b, preferred_element_type=F32)


def dot_t(a, b):
    return lax.dot_general(a, b, (((1,), (1,)), ((), ())), preferred_element_type=F32)


def first_kernel(merging, heads, taps_count, slab, *refs):
    if merging:
        x_ref, rim_ref, merge_ref, *refs = refs
    else:
        x_ref, rim_ref, *refs = refs
        merge_ref = None
    (gain_ref, value_ref, scans_ref, steps_ref, kernel_ref, taps_ref, bias_ref, decay_ref, *refs) = refs
    if merging:
        merged_ref, *refs = refs
    (xv_ref, bc_ref, pack_ref, prefix_ref, ext_ref, raw, state, scaled, before, total) = refs
    step = pl.program_id(0)
    inner = value_ref.shape[1]
    both = scans_ref.shape[1]
    state_n = both // 2
    padded = steps_ref.shape[0]

    def project(rows):
        if merging:
            rows = dot(rows, merge_ref[...]).astype(BF16)
        normed = rms(rows.astype(F32), gain_ref[...]).astype(BF16)
        return rows, normed

    def rounded(normed, weight):
        return dot(normed, weight).astype(BF16).astype(F32)

    @pl.when(step == 0)
    def _():
        _, normed = project(rim_ref[...])
        raw[0:8, :inner] = rounded(normed, value_ref[...])[RIM - 8 :]
        raw[0:8, inner:] = rounded(normed, scans_ref[...])[RIM - 8 :]
        state[...] = jnp.zeros_like(state)
        before[...] = jnp.zeros_like(before)
        total[...] = jnp.zeros_like(total)

    @pl.when(step > 0)
    def _():
        raw[0:8, :] = raw[BLOCK : BLOCK + 8, :]

    rows, normed = project(x_ref[...])
    if merging:
        merged_ref[...] = rows
    raw[8 : 8 + BLOCK, :inner] = rounded(normed, value_ref[...])
    raw[8 : 8 + BLOCK, inner:] = rounded(normed, scans_ref[...])

    def convolved(start, width, taps):
        summed = None
        for k in range(taps_count):
            at = 8 - (taps_count - 1) + k
            term = raw[at : at + BLOCK, start : start + width] * taps[k : k + 1, :]
            summed = term if summed is None else summed + term
        return silu(summed).astype(BF16)

    for start in range(0, both, LANES):
        bc_ref[:, start : start + LANES] = convolved(
            inner + start, LANES, taps_ref[:, start : start + LANES]
        )

    raw_steps = dot_t(steps_ref[...], normed) + bias_ref[:, 0:1]
    sizes = jnp.maximum(raw_steps, 0.0) + jnp.log1p(jnp.exp(-jnp.abs(raw_steps)))
    logs = -sizes * decay_ref[:, 0:1]
    upper = (
        lax.broadcasted_iota(jnp.int32, (BLOCK, BLOCK), 0)
        <= lax.broadcasted_iota(jnp.int32, (BLOCK, BLOCK), 1)
    ).astype(F32)
    cumul = jnp.dot(logs, upper, preferred_element_type=F32, precision=lax.Precision.HIGHEST)
    last = cumul[:, BLOCK - 1 : BLOCK]
    tail = jnp.exp(last - cumul) * sizes
    pack_ref[0, 0:padded, :] = cumul
    pack_ref[0, padded : 2 * padded, :] = jnp.log(sizes) - cumul
    pack_ref[0, 2 * padded : 3 * padded, :] = cumul + before[:, 0:1]
    before[...] = before[...] + last
    tail_columns = to_columns(tail)
    last_row = to_columns(cumul)[BLOCK - 1 : BLOCK, :]
    total[...] = total[...] + last_row
    kept = jnp.exp(last_row)

    per, groups = head_groups(heads)
    width = per * HEAD_DIM
    for g in range(groups):
        lanes = slice(g * width, (g + 1) * width)
        values = convolved(g * width, width, kernel_ref[:, lanes])
        xv_ref[:, lanes] = values
        scaled[:, lanes] = (
            values.astype(F32) * over_lanes(tail_columns, g * per, per)
        ).astype(BF16)
    prefix_ref[0] = state[...].astype(BF16)
    local = lax.dot_general(
        bc_ref[:, :state_n], scaled[...], (((0,), (0,)), ((), ())), preferred_element_type=F32
    )
    for g in range(groups):
        lanes = slice(g * width, (g + 1) * width)
        state[:, lanes] = state[:, lanes] * over_lanes(kept, g * per, per) + local[:, lanes]

    @pl.when(step == pl.num_programs(0) - 1)
    def _():
        ext_ref[:, :inner] = state[...].astype(BF16)
        part = lax.broadcasted_iota(jnp.int32, (state_n, LANES), 0) % slab
        sums = jnp.broadcast_to(total[...], (state_n, LANES))
        high = sums.astype(BF16).astype(F32)
        middle = (sums - high).astype(BF16).astype(F32)
        low = sums - high - middle
        ext_ref[:, inner:] = jnp.where(
            part == 0, high, jnp.where(part == 1, middle, jnp.where(part == 2, low, 0.0))
        ).astype(BF16)


def second_kernel(heads, stream_ref, gain_ref, gate_ref, xv_ref, bc_ref, pack_ref, prefix_ref, sg_ref, mixed_ref):
    state_n = bc_ref.shape[1] // 2
    padded = pack_ref.shape[1] // 3
    normed = rms(stream_ref[...].astype(F32), gain_ref[...]).astype(BF16)
    gate_rows = dot(normed, gate_ref[...]).astype(BF16).astype(F32)
    sg_ref[...] = silu(gate_rows).astype(BF16)
    b_map, c_map = bc_ref[:, :state_n], bc_ref[:, state_n:]
    lower = lax.broadcasted_iota(jnp.int32, (BLOCK, BLOCK), 0) >= lax.broadcasted_iota(
        jnp.int32, (BLOCK, BLOCK), 1
    )
    scores = jnp.where(lower, dot_t(c_map, b_map), 0.0)
    columns = to_columns(pack_ref[0, 0:padded, :])
    grown = jnp.exp(columns)
    earlier = dot(c_map, prefix_ref[0])
    per, groups = head_groups(heads)
    width = per * HEAD_DIM
    lane = lax.broadcasted_iota(jnp.int32, (BLOCK, width), 1)
    for g in range(groups):
        lanes = slice(g * width, (g + 1) * width)
        values = xv_ref[:, lanes]
        intra = None
        for k in range(per):
            h = g * per + k
            spread = columns[:, h : h + 1] + pack_ref[0, padded + h : padded + h + 1, :]
            weights = (jnp.exp(jnp.where(lower, spread, -1e30)) * scores).astype(BF16)
            piece = dot(weights, values)
            intra = piece if k == 0 else jnp.where(lane >= k * HEAD_DIM, piece, intra)
        mixed_ref[:, lanes] = (
            intra + earlier[:, lanes] * over_lanes(grown, g * per, per)
        ).astype(BF16)


def third_kernel(heads, finish, tiling, inner_total, stream_ref, sg_ref, mixed_ref, c_ref, pack_ref, incoming_ref, norm_ref, output_ref, *refs):
    padded = pack_ref.shape[1] // 3
    if finish:
        out_ref, gated_s, *hidden_s = refs
    else:
        out_ref, squares_ref, gated_s = refs
    grown = jnp.exp(to_columns(pack_ref[0, 2 * padded : 3 * padded, :]))
    carried = dot(c_ref[...], incoming_ref[...])
    per, groups = head_groups(heads)
    width = per * HEAD_DIM
    squares = None
    for g in range(groups):
        lanes = slice(g * width, (g + 1) * width)
        mixed = mixed_ref[:, lanes].astype(F32) + carried[:, lanes] * over_lanes(grown, g * per, per)
        gated = mixed * sg_ref[:, lanes].astype(F32)
        squares = gated * gated if squares is None else squares + gated * gated
        gated_s[:, lanes] = (gated * norm_ref[:, lanes]).astype(BF16)
    squares = jnp.sum(squares, axis=1, keepdims=True)
    branch = dot(gated_s[...], output_ref[...])
    if not finish:
        out_ref[...] = branch
        squares_ref[...] = jnp.broadcast_to(squares, (BLOCK, LANES))
        return
    branch = branch * lax.rsqrt(squares / inner_total + EPSILON)
    result = stream_ref[...].astype(F32) + branch
    if not tiling:
        out_ref[...] = result.astype(BF16)
        return
    hidden = hidden_s[0]
    features = result.shape[1]
    half = ROW_PATCHES // 2
    for c in range(features // LANES):
        hidden[c] = result[:, c * LANES : (c + 1) * LANES]
    for pair in range(BLOCK // (2 * ROW_PATCHES)):
        for i in range(2):
            for j in range(2):
                start = (2 * pair + i) * ROW_PATCHES + j
                for c in range(features // LANES):
                    at = (2 * i + j) * features + c * LANES
                    out_ref[pair * half : (pair + 1) * half, at : at + LANES] = hidden[
                        c, pl.ds(start, half, stride=2), :
                    ].astype(BF16)


def prefix_kernel(ext_ref, out_ref):
    count, slab, inner = out_ref.shape
    sums = jnp.sum(ext_ref[:, :, inner:].astype(F32), axis=1)
    spread = (
        lax.broadcasted_iota(jnp.int32, (LANES, inner), 0)
        == lax.broadcasted_iota(jnp.int32, (LANES, inner), 1) // HEAD_DIM
    ).astype(F32)
    kept = jnp.dot(
        jnp.exp(sums), spread, preferred_element_type=F32, precision=lax.Precision.HIGHEST
    )
    carried = jnp.zeros((slab, inner), F32)
    for k in range(count):
        out_ref[k] = carried.astype(BF16)
        carried = carried * kept[k : k + 1, :] + ext_ref[k, :, :inner].astype(F32)


def passed_along(block, axis, distance):
    devices = range(lax.axis_size(axis))
    route = [(i - distance, i) for i in devices if i - distance in devices]
    return lax.ppermute(block, axis, route)


def mamba(
    rows,
    merge_weight,
    gain_vec,
    gate_weight,
    value_weight,
    scan_weight,
    step_weight,
    kernel_value,
    kernel_scan,
    step_bias,
    decay_rate,
    norm_gain,
    out_weight,
    tiling,
):
    length, wide = rows.shape
    inner = value_weight.shape[1]
    heads = step_weight.shape[1]
    both = scan_weight.shape[1]
    state_n = both // 2
    taps_count = kernel_value.shape[0]
    features = out_weight.shape[1]
    blocks = length // BLOCK
    seq, shares = lax.axis_size("seq"), lax.axis_size("head")
    slab = state_n // seq
    padded = -(-heads // 8) * 8
    merging = merge_weight is not None
    extra = padded - heads
    steps_t = jnp.pad(step_weight.T, ((0, extra), (0, 0)))
    bias = jnp.broadcast_to(jnp.pad(step_bias, (0, extra))[:, None], (padded, LANES))
    decay = jnp.broadcast_to(jnp.pad(decay_rate, (0, extra))[:, None], (padded, LANES))
    gain = gain_vec[None, :]
    rim = passed_along(rows[length - RIM :], "seq", 1)

    shape = jax.ShapeDtypeStruct
    ins = [rows, rim] + ([merge_weight] if merging else [])
    ins += [gain, value_weight, scan_weight, steps_t, kernel_value, kernel_scan, bias, decay]
    outs = [shape((length, features), BF16)] if merging else []
    out_specs = [rows_of(features)] if merging else []
    outs += [
        shape((length, inner), BF16),
        shape((length, both), BF16),
        shape((blocks, 3 * padded, BLOCK), F32),
        shape((blocks, state_n, inner), BF16),
        shape((state_n, inner + LANES), BF16),
    ]
    pack_spec = pl.BlockSpec((1, 3 * padded, BLOCK), lambda i: (i, 0, 0))
    prefix_spec = pl.BlockSpec((1, state_n, inner), lambda i: (i, 0, 0))
    out_specs += [
        rows_of(inner),
        rows_of(both),
        pack_spec,
        prefix_spec,
        whole((state_n, inner + LANES)),
    ]
    made = pl.pallas_call(
        functools.partial(first_kernel, merging, heads, taps_count, slab),
        grid=(blocks,),
        in_specs=[rows_of(wide)] + [whole(a.shape) for a in ins[1:]],
        out_specs=out_specs,
        out_shape=outs,
        scratch_shapes=[
            pltpu.VMEM((BLOCK + 8, inner + both), F32),
            pltpu.VMEM((state_n, inner), F32),
            pltpu.VMEM((BLOCK, inner), BF16),
            pltpu.VMEM((padded, LANES), F32),
            pltpu.VMEM((1, LANES), F32),
        ],
        compiler_params=params(),
        name="first_merge" if merging else "first",
    )(*ins)
    stream = made[0] if merging else rows
    xv, bc, pack, prefix, ext = made[-5:]

    spread_out = lax.all_to_all(
        ext.reshape(seq, slab, inner + LANES), "seq", 0, 0, tiled=True
    )

    flops = 2 * length * (features * inner + inner * (BLOCK * 4 + state_n) + BLOCK * state_n)
    sg, mixed = pl.pallas_call(
        functools.partial(second_kernel, heads),
        grid=(blocks,),
        in_specs=[
            rows_of(features),
            whole(gain.shape),
            whole(gate_weight.shape),
            rows_of(inner),
            rows_of(both),
            pack_spec,
            prefix_spec,
        ],
        out_specs=[rows_of(inner), rows_of(inner)],
        out_shape=[shape((length, inner), BF16), shape((length, inner), BF16)],
        compiler_params=params(),
        cost_estimate=pl.CostEstimate(
            flops=flops, bytes_accessed=12 * length * inner, transcendentals=length * heads * BLOCK
        ),
        name="second",
    )(stream, gain, gate_weight, xv, bc, pack, prefix)

    before = pl.pallas_call(
        prefix_kernel,
        out_shape=shape((seq, slab, inner), BF16),
        in_specs=[pl.BlockSpec(memory_space=pltpu.VMEM)],
        out_specs=pl.BlockSpec(memory_space=pltpu.VMEM),
        compiler_params=pltpu.CompilerParams(vmem_limit_bytes=VMEM_LIMIT),
        name="prefix",
    )(spread_out)
    incoming = lax.all_to_all(before, "seq", 0, 0, tiled=True).reshape(state_n, inner)

    norm = norm_gain[None, :]
    finish = shares == 1
    scratch = [pltpu.VMEM((BLOCK, inner), BF16)]
    if not finish:
        outs = [shape((length, features), F32), shape((length, LANES), F32)]
        out_specs = [rows_of(features), rows_of(LANES)]
    elif tiling:
        outs = shape((length // 4, 4 * features), BF16)
        out_specs = pl.BlockSpec((BLOCK // 4, 4 * features), lambda i: (i, 0))
        scratch += [pltpu.VMEM((features // LANES, BLOCK, LANES), F32)]
    else:
        outs, out_specs = shape((length, features), BF16), rows_of(features)
    result = pl.pallas_call(
        functools.partial(third_kernel, heads, finish, tiling, inner * shares),
        grid=(blocks,),
        in_specs=[
            rows_of(features),
            rows_of(inner),
            rows_of(inner),
            pl.BlockSpec((BLOCK, state_n), lambda i: (i, 1)),
            pack_spec,
            whole((state_n, inner)),
            whole(norm.shape),
            whole(out_weight.shape),
        ],
        out_specs=out_specs,
        out_shape=outs,
        scratch_shapes=scratch,
        compiler_params=params(),
        name="third_tiles" if tiling else "third",
    )(stream, sg, mixed, bc, pack, incoming, norm, out_weight)
    if finish:
        return result
    branch, squares = result
    mean = lax.psum(squares[:, :1], "head") / (inner * shares)
    branch = (branch * lax.rsqrt(mean + EPSILON)).astype(BF16)
    if tiling:
        summed = lax.psum(branch, "head").astype(F32)
        return merge_tiles((stream.astype(F32) + summed).astype(BF16))
    summed = lax.psum_scatter(branch, "head", scatter_dimension=1, tiled=True).astype(F32)
    share = features // shares
    mine = lax.dynamic_slice_in_dim(stream, lax.axis_index("head") * share, share, 1)
    return (mine.astype(F32) + summed).astype(BF16)


def merge_tiles(rows):
    count, width_here = rows.shape
    grid = rows.reshape(count // (2 * ROW_PATCHES), 2, ROW_PATCHES // 2, 2, width_here)
    return grid.transpose(0, 2, 1, 3, 4).reshape(count // 4, 4 * width_here)


def shards(tokens, *weights):
    tiles = mamba(tokens, None, *weights[:11], True)
    return mamba(tiles, weights[11], *weights[12:], False)


def solution(mesh):
    return jax.shard_map(
        shards,
        mesh=mesh,
        in_specs=(
            P("seq", None),
            P(),
            P(None, "head"),
            P(None, "head"),
            P(),
            P(None, "head"),
            P(None, "head"),
            P(),
            P("head"),
            P("head"),
            P("head"),
            P("head", None),
            P(),
            P(),
            P(None, "head"),
            P(None, "head"),
            P(),
            P(None, "head"),
            P(None, "head"),
            P(),
            P("head"),
            P("head"),
            P("head"),
            P("head", None),
        ),
        out_specs=P("seq", "head"),
        check_vma=False,
    )
```

time: 718 us -> 226 us (0.31)
  other arithmetic: 235 us -> 0 us
  waiting for transfers between devices: 157 us -> 7.98 us
  Pallas kernels: 0 us -> 136 us
  matrix products: 108 us -> 0 us
  local copies, waits for them, and re-layouts: 101 us -> 12 us
  blocking collectives: 86.9 us -> 58.3 us
  between operations: 14.6 us -> 0.22 us
    all_gather x2 -> x0, waiting for transfers between devices: 156 us -> none  [carried_in(): lax.all_gather(part.astype(kind), axis)]
    pallas_call x0 -> x8, Pallas kernels: none -> 136 us  [the longest x2 65.7 us: mamba(): pl.pallas_call(functools.partial(first_kernel, merging, heads, taps_count...]
    dot_general x19 -> x0, matrix products: 108 us -> none  [the longest x2 26.5 us: local_scan(): jnp.einsum('ctn,chpn->cthp', c_blk.astype(jnp.float32), start_state, prec...]
    select_n x64 -> x0, other arithmetic: 106 us -> none  [lap(): return jax.tree.map(lambda a, b: jnp.where(reached, a, b), new, before)]
    unnamed x2 -> x0, blocking collectives: 86.9 us -> none
    convert_element_type x73 -> x0, other arithmetic: 65.2 us -> none  [the longest x2 41 us: mamba_local(): convolved = jax.nn.silu(summed).astype(jnp.bfloat16)]
    all_to_all x0 -> x2, blocking collectives: none -> 58.3 us  [mamba(): lax.all_to_all(ext.reshape(seq, slab, inner + LANES), 'seq', 0, 0, tiled=...]
    reshape x7 -> x0, local copies, waits for them, and re-layouts: 52.4 us -> none  [the longest x2 31.3 us: local_scan(): return (intra + inter).reshape(length, heads_here * HEAD_DIM)]
  transfers between devices with their start and end apart: 4 -> 4, of which waited for: 3 -> 3; matrix products, arithmetic and copies ran while one was open for 6% -> 0% of each run, Pallas kernels for 0% -> 17%
where the time goes in v1:
time: 226 us; the launch traced here: 225 us
  Pallas kernels  136 us (60%)
  blocking collectives  58.3 us (26%)
  local copies, waits for them, and re-layouts  12 us (5%)
  starting transfers between devices  9.97 us (4%)
  waiting for transfers between devices  7.98 us (4%)
    pallas_call x2, Pallas kernels, mamba(): pl.pallas_call(functools.partial(first_kernel, merging, heads, taps_count...  65.7 us
    all_to_all x2, blocking collectives, mamba(): lax.all_to_all(ext.reshape(seq, slab, inner + LANES), 'seq', 0, 0, tiled=...  58.3 us
    pallas_call x2, Pallas kernels, mamba(): pl.pallas_call(functools.partial(second_kernel, heads), grid=(blocks,), i...  38.1 us
    pallas_call x2, Pallas kernels, mamba(): pl.pallas_call(functools.partial(third_kernel, heads, finish, tiling, inn...  29.9 us
    unnamed x48, local copies, waits for them, and re-layouts  9.74 us
    all_to_all x2, waiting for transfers between devices, mamba(): lax.all_to_all(before, 'seq', 0, 0, tiled=True).reshape(state_n, inner)  6.51 us
    all_to_all x2, starting transfers between devices, mamba(): lax.all_to_all(before, 'seq', 0, 0, tiled=True).reshape(state_n, inner)  5.45 us
    ppermute x2, starting transfers between devices, passed_along(): return lax.ppermute(block, axis, route)  4.52 us
  transfers between devices with their start and end apart: 4, of which 3 were waited for; matrix products, arithmetic and copies ran while one was open for 0% of the time, Pallas kernels for 17%

profile of v1, /device:TPU:0, one launch (start us, length us, event | category | flops | bytes accessed | tf_op | source)
XLA Modules:
  0.0 224.7 jit_solution(17117232984579314537)
XLA Ops:
  0.0 0.7 slice.6
  0.7 2.3 %collective-permute-start = (bf16[16,256]{1,0:T(8,128)(2,1)S(1)}, bf16[16,256]{1,0:T(8,128)(2,1)S(1)}, u32[]{:S(2)}, u32[]{:S(2)}) collective-permute-start(bf16[16,256]{1,0:T(8,128)(2,1)S(1)} %slice.6), channel_id=1, source_target_pairs={{0,1},{1,2},{2,3},{3,4},{4,5},{5,6},{6,7},{7,8},{8,9},{9,10},{10,1... | collective-permute-start | bytes 24584 | tf_op jit(solution)/shard_map/ppermute | solution.py:278
  3.1 0.8 collective-permute-done.refs_1_
  3.9 0.7 broadcast_in_dim.17.refs_8_
  4.6 0.7 broadcast_in_dim.18.refs_9_
  5.3 1.6 copy-done.1
  6.9 0.9 copy-done.8
  7.9 0.9 copy-done.9
  8.8 0.7 copy-done.12
  9.5 0.7 copy-done.13
  10.2 0.7 copy-done.17
  10.9 0.7 copy-done.19
  11.6 33.9 %first.1 = (bf16[4096,512]{1,0:T(8,128)(2,1)}, bf16[4096,512]{1,0:T(8,128)(2,1)}, f32[16,24,256]{2,1,0:T(8,128)S(1)}, bf16[16,256,512]{2,1,0:T(8,128)(2,1)}, bf16[256,640]{1,0:T(8,128)(2,1)S(1)}) custom-call(bf16[4096,256]{1,0:T(8,128)(2,1)S(1)} %copy-done.1, bf16[16,256]{1,0:T(8,128)(2,1)S(1)} %collective-permute-done.refs_1_, f32[1,256]{1,0:T(1,128)S(1)} %bitcast.20, ...), custom_call_target="tpu_custom_call" | custom-call | tf_op jit(solution)/shard_map/first/pallas_call | solution.py:337
  45.5 20.9 %all_to_all.20.ext_ref = bf16[32,8,640]{2,1,0:T(8,128)(2,1)S(1)} all-to-all(bf16[32,8,640]{2,1,0:T(8,128)(2,1)S(1)} %bitcast.13), channel_id=1, replica_groups=mesh['seq'=32,'head'=1] {'seq'}, dimensions={0} | all-to-all | bytes 655360 | tf_op jit(solution)/shard_map/all_to_all | solution.py:356
  66.3 1.0 prefix.2
  67.4 2.6 %all-to-all-start.1 = ((bf16[32,8,512]{2,1,0:T(8,128)(2,1)}), bf16[32,8,512]{2,1,0:T(8,128)(2,1)S(1)}, u32[]{:S(2)}, u32[]{:S(2)}) async-start(bf16[32,8,512]{2,1,0:T(8,128)(2,1)} %prefix.2), calls=%async_computation.1 | async-start | bytes 524288 | tf_op jit(solution)/shard_map/all_to_all | solution.py:390
  70.0 0.0 copy-done.20
  70.0 0.0 copy-done.2
  70.0 0.0 copy-done.21
  70.0 0.0 copy-start.7
  70.0 0.0 copy-start.18
  70.0 19.8 %second.2 = (bf16[4096,512]{1,0:T(8,128)(2,1)}, bf16[4096,512]{1,0:T(8,128)(2,1)}) custom-call(bf16[4096,256]{1,0:T(8,128)(2,1)S(1)} %copy-done.2, f32[1,256]{1,0:T(1,128)S(1)} %bitcast.21, bf16[256,512]{1,0:T(8,128)(2,1)S(1)} %copy-done.21, bf16[4096,512]{1,0:T(8,128)(2,1)} %get-tuple-element.20.xv_ref, bf16[4096,512]{1,0:T(8,128)(2,1)} %get-tuple-element.21.bc_ref.c_ref, ...), custom_call_target="tpu_custom_call" | custom-call | flops 6979321856 | bytes 25165824 | tf_op jit(solution)/shard_map/second/pallas_call | solution.py:361
  89.8 0.0 all-to-all-done.1
  89.8 0.0 copy-start.22
  89.9 0.0 copy-start.23
  89.9 0.0 copy-start.3
  89.9 0.0 copy-start.10
  89.9 0.0 copy-start.11
  89.9 0.0 copy-start.14
  89.9 0.0 copy-start.16
  89.9 15.9 %third_tiles.1.refs_0_ = bf16[1024,1024]{1,0:T(8,128)(2,1)S(1)} custom-call(bf16[4096,256]{1,0:T(8,128)(2,1)S(1)} %copy-done.2, bf16[4096,512]{1,0:T(8,128)(2,1)} %get-tuple-element.24.sg_ref, bf16[4096,512]{1,0:T(8,128)(2,1)} %get-tuple-element.25.mixed_ref, bf16[4096,512]{1,0:T(8,128)(2,1)} %get-tuple-element.21.bc_ref.c_ref, ...), custom_call_target="tpu_custom_call" | custom-call | tf_op jit(solution)/shard_map/third_tiles/pallas_call | solution.py:404
  105.9 0.0 copy-start
  105.9 2.2 collective-permute-start.1
  108.1 0.7 collective-permute-done.1.refs_1_
  108.7 0.1 broadcast_in_dim.41.refs_9_
  108.8 0.0 copy-done.23
  108.8 0.1 broadcast_in_dim.42.refs_10_
  108.9 31.8 %first_merge.1 = (bf16[1024,1024]{1,0:T(8,128)(2,1)S(1)}, bf16[1024,2048]{1,0:T(8,128)(2,1)}, bf16[1024,512]{1,0:T(8,128)(2,1)S(1)}, f32[4,96,256]{2,1,0:T(8,128...) custom-call(bf16[1024,1024]{1,0:T(8,128)(2,1)} %copy-done, ...), custom_call_target="tpu_custom_call" | custom-call | tf_op jit(solution)/shard_map/first_merge/pallas_call | solution.py:337
  140.7 1.0 copy-done.4
  141.7 37.4 %all_to_all.21.ext_ref = bf16[32,8,2176]{2,1,0:T(8,128)(2,1)S(1)} all-to-all(bf16[32,8,2176]{2,1,0:T(8,128)(2,1)S(1)} %bitcast.11), channel_id=1, replica_groups=mesh['seq'=32,'head'=1] {'seq'}, dimensions={0} | all-to-all | bytes 2228224 | tf_op jit(solution)/shard_map/all_to_all | solution.py:356
  179.1 1.6 prefix.3
  180.6 2.9 %all-to-all-start.3 = ((bf16[32,8,2048]{2,1,0:T(8,128)(2,1)}), bf16[32,8,2048]{2,1,0:T(8,128)(2,1)S(1)}, u32[]{:S(2)}, u32[]{:S(2)}) async-start(bf16[32,8,2048]{2,1,0:T(8,128)(2,1)} %prefix.3), calls=%async_computation.3 | async-start | bytes 2097152 | tf_op jit(solution)/shard_map/all_to_all | solution.py:390
  183.5 0.0 copy-start.5
  183.5 1.2 copy-done.5
  184.7 18.3 %second.3 = (bf16[1024,2048]{1,0:T(8,128)(2,1)}, bf16[1024,2048]{1,0:T(8,128)(2,1)}) custom-call(bf16[1024,1024]{1,0:T(8,128)(2,1)S(1)} %get-tuple-element.27.stream_ref, f32[1,1024]{1,0:T(1,128)S(1)} %bitcast.17, bf16[1024,2048]{1,0:T(8,128)(2,1)} %gate_ref.3, bf16[1024,2048]{1,0:T(8,128)(2,1)} %get-tuple-element.28.xv_ref, ...), custom_call_target="tpu_custom_call" | custom-call | flops 9797894144 | bytes 25165824 | tf_op jit(solution)/shard_map/second/pallas_call | solution.py:361
  203.0 6.5 %all-to-all-done.3 = bf16[32,8,2048]{2,1,0:T(8,128)(2,1)S(1)} async-done(((bf16[32,8,2048]{2,1,0:T(8,128)(2,1)}), bf16[32,8,2048]{2,1,0:T(8,128)(2,1)S(1)}, u32[]{:S(2)}, u32[]{:S(2)}) %all-to-all-start.3) | async-done | bytes 1048608 | tf_op jit(solution)/shard_map/all_to_all | solution.py:390
  209.5 1.2 copy-done.6
  210.7 13.9 %third.1 = bf16[1024,1024]{1,0:T(8,128)(2,1)} custom-call(bf16[1024,1024]{1,0:T(8,128)(2,1)S(1)} %get-tuple-element.27.stream_ref, bf16[1024,2048]{1,0:T(8,128)(2,1)} %get-tuple-element.32.sg_ref, bf16[1024,2048]{1,0:T(8,128)(2,1)} %get-tuple-element.33.mixed_ref, bf16[1024,512]{1,0:T(8,128)(2,1)S(1)} %copy-done.6, ...), custom_call_target="tpu_custom_call" | custom-call | tf_op jit(solution)/shard_map/third/pallas_call | solution.py:404
  (24 shorter events, 0.0 us)
Async XLA Ops:
  0.0 70.0 %copy-start.20 = (f32[256]{0:T(256)S(1)}, f32[256]{0:T(256)}, u32[]{:S(2)}) copy-start(f32[256]{0:T(256)} %param.25) | copy-start | bytes 3076
  0.7 3.2 %collective-permute-start = (bf16[16,256]{1,0:T(8,128)(2,1)S(1)}, bf16[16,256]{1,0:T(8,128)(2,1)S(1)}, u32[]{:S(2)}, u32[]{:S(2)}) collective-permute-start(bf16[16,256]{1,0:T(8,128)(2,1)S(1)} %slice.6), channel_id=1, source_target_pairs={{0,1},{1,2},{2,3},{3,4},{4,5},{5,6},{6,7},{7,8},{8,9},{9,10},{10,1... | collective-permute-start | bytes 24584 | tf_op jit(solution)/shard_map/ppermute | solution.py:278
  5.3 1.6 copy-start.1
  6.9 0.9 copy-start.8
  7.9 0.9 copy-start.9
  8.8 0.7 copy-start.12
  9.5 0.7 copy-start.13
  10.2 0.7 copy-start.17
  10.9 0.7 copy-start.19
  11.6 58.4 %copy-start.2 = (bf16[4096,256]{1,0:T(8,128)(2,1)S(1)}, bf16[4096,256]{1,0:T(8,128)(2,1)}, u32[]{:S(2)}) copy-start(bf16[4096,256]{1,0:T(8,128)(2,1)} %stream_ref.3) | copy-start | bytes 6291460
  11.6 58.4 %copy-start.21 = (bf16[256,512]{1,0:T(8,128)(2,1)S(1)}, bf16[256,512]{1,0:T(8,128)(2,1)}, u32[]{:S(2)}) copy-start(bf16[256,512]{1,0:T(8,128)(2,1)} %gate_ref.2) | copy-start | bytes 786436
  67.4 22.4 %all-to-all-start.1 = ((bf16[32,8,512]{2,1,0:T(8,128)(2,1)}), bf16[32,8,512]{2,1,0:T(8,128)(2,1)S(1)}, u32[]{:S(2)}, u32[]{:S(2)}) async-start(bf16[32,8,512]{2,1,0:T(8,128)(2,1)} %prefix.2), calls=%async_computation.1 | async-start | bytes 524288 | tf_op jit(solution)/shard_map/all_to_all | solution.py:390
  70.0 19.8 %copy-start.7 = (bf16[512,256]{1,0:T(8,128)(2,1)S(1)}, bf16[512,256]{1,0:T(8,128)(2,1)}, u32[]{:S(2)}) copy-start(bf16[512,256]{1,0:T(8,128)(2,1)} %output_ref.2) | copy-start | bytes 786436
  70.0 19.8 %copy-start.18 = (f32[512]{0:T(512)S(1)}, f32[512]{0:T(512)}, u32[]{:S(2)}) copy-start(f32[512]{0:T(512)} %param.34) | copy-start | bytes 6148
  89.8 18.9 %copy-start.22 = (f32[32]{0:T(128)S(1)}, f32[32]{0:T(128)}, u32[]{:S(2)}) copy-start(f32[32]{0:T(128)} %param.44) | copy-start | bytes 388
  89.9 19.0 %copy-start.23 = (f32[32]{0:T(128)S(1)}, f32[32]{0:T(128)}, u32[]{:S(2)}) copy-start(f32[32]{0:T(128)} %param.45) | copy-start | bytes 388
  89.9 19.0 %copy-start.3 = (bf16[1024,512]{1,0:T(8,128)(2,1)S(1)}, bf16[1024,512]{1,0:T(8,128)(2,1)}, u32[]{:S(2)}) copy-start(bf16[1024,512]{1,0:T(8,128)(2,1)} %refs_5_.1) | copy-start | bytes 3145732
  89.9 19.0 %copy-start.10 = (bf16[1024,32]{0,1:T(8,128)(2,1)S(1)}, bf16[1024,32]{0,1:T(8,128)(2,1)}, u32[]{:S(2)}) copy-start(bf16[1024,32]{0,1:T(8,128)(2,1)} %param.41) | copy-start | bytes 196612
  89.9 19.0 %copy-start.11 = (f32[4,2048]{1,0:T(4,128)S(1)}, f32[4,2048]{1,0:T(4,128)}, u32[]{:S(2)}) copy-start(f32[4,2048]{1,0:T(4,128)} %refs_7_.3) | copy-start | bytes 98308
  89.9 19.0 %copy-start.14 = (f32[4,512]{1,0:T(4,128)S(1)}, f32[4,512]{1,0:T(4,128)}, u32[]{:S(2)}) copy-start(f32[4,512]{1,0:T(4,128)} %refs_8_.1) | copy-start | bytes 24580
  89.9 19.0 %copy-start.16 = (f32[1024]{0:T(1024)S(1)}, f32[1024]{0:T(1024)}, u32[]{:S(2)}) copy-start(f32[1024]{0:T(1024)} %param.37) | copy-start | bytes 12292
  105.9 3.0 %copy-start = (bf16[1024,1024]{1,0:T(8,128)(2,1)}, bf16[1024,1024]{1,0:T(8,128)(2,1)S(1)}, u32[]{:S(2)}) copy-start(bf16[1024,1024]{1,0:T(8,128)(2,1)S(1)} %third_tiles.1.refs_0_) | copy-start | bytes 6291460
  105.9 2.8 %collective-permute-start.1 = (bf16[16,1024]{1,0:T(8,128)(2,1)S(1)}, bf16[16,1024]{1,0:T(8,128)(2,1)S(1)}, u32[]{:S(2)}, u32[]{:S(2)}) collective-permute-start(bf16[16,1024]{1,0:T(8,128)(2,1)S(1)} %slice.8), channel_id=1, source_target_pairs={{0,1},{1,2},{2,3},{3,4},{4,5},{5,6},{6,7},{7,8},{8,9},{9,10},{10,1... | collective-permute-start | bytes 98312 | tf_op jit(solution)/shard_map/ppermute | solution.py:278
  140.7 1.0 copy-start.4
  180.6 28.9 %all-to-all-start.3 = ((bf16[32,8,2048]{2,1,0:T(8,128)(2,1)}), bf16[32,8,2048]{2,1,0:T(8,128)(2,1)S(1)}, u32[]{:S(2)}, u32[]{:S(2)}) async-start(bf16[32,8,2048]{2,1,0:T(8,128)(2,1)} %prefix.3), calls=%async_computation.3 | async-start | bytes 2097152 | tf_op jit(solution)/shard_map/all_to_all | solution.py:390
  183.5 1.2 copy-start.5
  184.7 24.8 %copy-start.15 = (f32[2048]{0:T(1024)S(1)}, f32[2048]{0:T(1024)}, u32[]{:S(2)}) copy-start(f32[2048]{0:T(1024)} %param.46) | copy-start | bytes 24580
  209.5 1.2 copy-start.6

commit v2 on v1

--- a/solution.py
+++ b/solution.py
@@ -180,7 +180,8 @@
         ).astype(BF16)
 
 
-def second_kernel(heads, stream_ref, gain_ref, gate_ref, xv_ref, bc_ref, pack_ref, prefix_ref, sg_ref, mixed_ref):
+def second_kernel(heads, kept, *refs):
+    stream_ref, gain_ref, gate_ref, xv_ref, bc_ref, pack_ref, prefix_ref, sg_ref, mixed_ref = refs[kept:]
     state_n = bc_ref.shape[1] // 2
     padded = pack_ref.shape[1] // 3
     normed = rms(stream_ref[...].astype(F32), gain_ref[...]).astype(BF16)
@@ -358,26 +359,44 @@
     )
 
     flops = 2 * length * (features * inner + inner * (BLOCK * 4 + state_n) + BLOCK * state_n)
-    sg, mixed = pl.pallas_call(
-        functools.partial(second_kernel, heads),
-        grid=(blocks,),
-        in_specs=[
-            rows_of(features),
-            whole(gain.shape),
-            whole(gate_weight.shape),
-            rows_of(inner),
-            rows_of(both),
-            pack_spec,
-            prefix_spec,
-        ],
-        out_specs=[rows_of(inner), rows_of(inner)],
-        out_shape=[shape((length, inner), BF16), shape((length, inner), BF16)],
-        compiler_params=params(),
-        cost_estimate=pl.CostEstimate(
-            flops=flops, bytes_accessed=12 * length * inner, transcendentals=length * heads * BLOCK
-        ),
-        name="second",
-    )(stream, gain, gate_weight, xv, bc, pack, prefix)
+    def second(start, count, made):
+        def at(width):
+            return pl.BlockSpec((BLOCK, width), lambda i: (i + start, 0))
+
+        def at_block(spec):
+            return pl.BlockSpec(spec.block_shape, lambda i: (i + start, 0, 0))
+
+        kept = [pl.BlockSpec(memory_space=pl.ANY)] * len(made)
+        return pl.pallas_call(
+            functools.partial(second_kernel, heads, len(made)),
+            grid=(count,),
+            in_specs=kept
+            + [
+                at(features),
+                whole(gain.shape),
+                whole(gate_weight.shape),
+                at(inner),
+                at(both),
+                at_block(pack_spec),
+                at_block(prefix_spec),
+            ],
+            out_specs=[at(inner), at(inner)],
+            out_shape=[shape((length, inner), BF16), shape((length, inner), BF16)],
+            input_output_aliases={k: k for k in range(len(made))},
+            compiler_params=params(),
+            cost_estimate=pl.CostEstimate(
+                flops=flops * count // blocks,
+                bytes_accessed=12 * count * BLOCK * inner,
+                transcendentals=count * BLOCK * heads * BLOCK,
+            ),
+            name="second_rest" if made else "second",
+        )(*made, stream, gain, gate_weight, xv, bc, pack, prefix)
+
+    early = blocks // 2 if tiling else blocks
+    sg, mixed = second(0, early, [])
+    if early < blocks:
+        spread_out, sg, mixed = lax.optimization_barrier((spread_out, sg, mixed))
+        sg, mixed = second(early, blocks - early, [sg, mixed])
 
     before = pl.pallas_call(
         prefix_kernel,

time: 226 us -> 221 us (0.978)
  blocking collectives: 58.3 us -> 37.2 us
  starting transfers between devices: 9.97 us -> 22.5 us
    all_to_all x2 -> x1, blocking collectives: 58.3 us -> 37.2 us  [mamba(): lax.all_to_all(ext.reshape(seq, slab, inner + LANES), 'seq', 0, 0, tiled=...]
    all_to_all x0 -> x1, starting transfers between devices: none -> 9.1 us  [mamba(): lax.all_to_all(ext.reshape(seq, slab, inner + LANES), 'seq', 0, 0, tiled=...]
    all_to_all x2, starting transfers between devices: 5.45 us -> 8.7 us  [mamba(): lax.all_to_all(before, 'seq', 0, 0, tiled=True).reshape(state_n, inner)]
    pallas_call x2 -> x3, Pallas kernels: 38.1 us -> 39.7 us  [second(): pl.pallas_call(functools.partial(second_kernel, heads, len(made)), grid=(...]
    unnamed x48 -> x52, local copies, waits for them, and re-layouts: 9.74 us -> 11.4 us
  transfers between devices with their start and end apart: 4 -> 5, of which waited for: 3 -> 3; matrix products, arithmetic and copies ran while one was open for 0% -> 0% of each run, Pallas kernels for 17% -> 18%
where the time goes in v2:
time: 221 us; the launch traced here: 220 us
  Pallas kernels  138 us (62%)
  blocking collectives  37.2 us (17%)
  starting transfers between devices  22.5 us (10%)
  local copies, waits for them, and re-layouts  13.6 us (6%)
  waiting for transfers between devices  7.99 us (4%)
    pallas_call x2, Pallas kernels, mamba(): pl.pallas_call(functools.partial(first_kernel, merging, heads, taps_count...  65.8 us
    pallas_call x3, Pallas kernels, second(): pl.pallas_call(functools.partial(second_kernel, heads, len(made)), grid=(...  39.7 us
    all_to_all x1, blocking collectives, mamba(): lax.all_to_all(ext.reshape(seq, slab, inner + LANES), 'seq', 0, 0, tiled=...  37.2 us
    pallas_call x2, Pallas kernels, mamba(): pl.pallas_call(functools.partial(third_kernel, heads, finish, tiling, inn...  29.9 us
    unnamed x52, local copies, waits for them, and re-layouts  11.4 us
    all_to_all x1, starting transfers between devices, mamba(): lax.all_to_all(ext.reshape(seq, slab, inner + LANES), 'seq', 0, 0, tiled=...  9.1 us
    all_to_all x2, starting transfers between devices, mamba(): lax.all_to_all(before, 'seq', 0, 0, tiled=True).reshape(state_n, inner)  8.7 us
    all_to_all x2, waiting for transfers between devices, mamba(): lax.all_to_all(before, 'seq', 0, 0, tiled=True).reshape(state_n, inner)  6.52 us
  transfers between devices with their start and end apart: 5, of which 3 were waited for; matrix products, arithmetic and copies ran while one was open for 0% of the time, Pallas kernels for 18%

profile of v2, /device:TPU:0, one launch (start us, length us, event | category | flops | bytes accessed | tf_op | source)
XLA Modules:
  0.0 219.6 jit_solution(7788073180014819507)
XLA Ops:
  0.0 0.7 slice.6
  0.7 2.3 %collective-permute-start = (bf16[16,256]{1,0:T(8,128)(2,1)S(1)}, bf16[16,256]{1,0:T(8,128)(2,1)S(1)}, u32[]{:S(2)}, u32[]{:S(2)}) collective-permute-start(bf16[16,256]{1,0:T(8,128)(2,1)S(1)} %slice.6), channel_id=1, source_target_pairs={{0,1},{1,2},{2,3},{3,4},{4,5},{5,6},{6,7},{7,8},{8,9},{9,10},{10,1... | collective-permute-start | bytes 24584 | tf_op jit(solution)/shard_map/ppermute | solution.py:279
  3.1 0.8 collective-permute-done.refs_1_
  3.9 0.7 broadcast_in_dim.17.refs_8_
  4.6 0.7 broadcast_in_dim.18.refs_9_
  5.3 1.6 copy-done
  6.9 0.9 copy-done.10
  7.9 0.9 copy-done.11
  8.8 0.7 copy-done.14
  9.5 0.7 copy-done.17
  10.2 0.7 copy-done.18
  10.9 0.7 copy-done.22
  11.6 34.0 %first.1 = (bf16[4096,512]{1,0:T(8,128)(2,1)}, bf16[4096,512]{1,0:T(8,128)(2,1)}, f32[16,24,256]{2,1,0:T(8,128)S(1)}, bf16[16,256,512]{2,1,0:T(8,128)(2,1)}, bf16[256,640]{1,0:T(8,128)(2,1)}) custom-call(bf16[4096,256]{1,0:T(8,128)(2,1)S(1)} %copy-done, bf16[16,256]{1,0:T(8,128)(2,1)S(1)} %collective-permute-done.refs_1_, f32[1,256]{1,0:T(1,128)S(1)} %bitcast.14, ...), custom_call_target="tpu_custom_call" | custom-call | tf_op jit(solution)/shard_map/first/pallas_call | solution.py:338
  45.6 9.1 %all-to-all-start = ((bf16[32,8,640]{2,1,0:T(8,128)(2,1)}), bf16[32,8,640]{2,1,0:T(8,128)(2,1)S(1)}, u32[]{:S(2)}, u32[]{:S(2)}) async-start(bf16[32,8,640]{2,1,0:T(8,128)(2,1)} %bitcast.2), calls=%async_computation | async-start | bytes 655360 | tf_op jit(solution)/shard_map/all_to_all | solution.py:357
  54.7 0.0 copy-start.3
  54.7 0.9 copy-done.3
  55.7 0.7 copy-done.15
  56.3 10.7 %second.2 = (bf16[4096,512]{1,0:T(8,128)(2,1)}, bf16[4096,512]{1,0:T(8,128)(2,1)}) custom-call(bf16[4096,256]{1,0:T(8,128)(2,1)S(1)} %copy-done.1, f32[1,256]{1,0:T(1,128)S(1)} %bitcast.15, bf16[256,512]{1,0:T(8,128)(2,1)S(1)} %copy-done.3, bf16[4096,512]{1,0:T(8,128)(2,1)} %get-tuple-element.26.refs_3_.refs_5_, ...), custom_call_target="tpu_custom_call" | custom-call | flops 3489660928 | bytes 12582912 | tf_op jit(solution)/shard_map/second/pallas_call | solution.py:370
  67.1 0.0 all-to-all-done.ext_ref
  67.1 1.0 prefix.2
  68.1 5.8 %all-to-all-start.1 = ((bf16[32,8,512]{2,1,0:T(8,128)(2,1)}), bf16[32,8,512]{2,1,0:T(8,128)(2,1)S(1)}, u32[]{:S(2)}, u32[]{:S(2)}) async-start(bf16[32,8,512]{2,1,0:T(8,128)(2,1)} %prefix.2), calls=%async_computation.1 | async-start | bytes 524288 | tf_op jit(solution)/shard_map/all_to_all | solution.py:409
  74.0 0.0 copy-start.9
  74.0 0.0 copy-start.23
  74.0 10.7 %second_rest.1 = (bf16[4096,512]{1,0:T(8,128)(2,1)}, bf16[4096,512]{1,0:T(8,128)(2,1)}) custom-call(bf16[4096,512]{1,0:T(8,128)(2,1)} %get-tuple-element.32.refs_0_, bf16[4096,512]{1,0:T(8,128)(2,1)} %get-tuple-element.33.refs_1_, bf16[4096,256]{1,0:T(8,128)(2,1)S(1)} %copy-done.1, ...), custom_call_target="tpu_custom_call", output_to_operand_aliasing={{0}: (0, {}), {1}: (1, {})} | custom-call | flops 3489660928 | bytes 12582912 | tf_op jit(solution)/shard_map/second_rest/pallas_call | solution.py:370
  84.8 0.0 copy-start.24
  84.8 0.0 copy-start.25
  84.8 0.0 copy-start.5
  84.8 0.0 copy-start.12
  84.8 0.0 copy-start.13
  84.8 0.0 copy-start.19
  84.9 0.0 copy-start.21
  84.9 15.9 %third_tiles.1.refs_0_ = bf16[1024,1024]{1,0:T(8,128)(2,1)S(1)} custom-call(bf16[4096,256]{1,0:T(8,128)(2,1)S(1)} %copy-done.1, bf16[4096,512]{1,0:T(8,128)(2,1)} %get-tuple-element.34.sg_ref, bf16[4096,512]{1,0:T(8,128)(2,1)} %get-tuple-element.35.mixed_ref, bf16[4096,512]{1,0:T(8,128)(2,1)} %get-tuple-element.27.refs_4_.refs_6_.c_ref, ...), custom_call_target="tpu_custom_call" | custom-call | tf_op jit(solution)/shard_map/third_tiles/pallas_call | solution.py:423
  100.8 0.0 copy-start.2
  100.8 2.3 %collective-permute-start.1 = (bf16[16,1024]{1,0:T(8,128)(2,1)S(1)}, bf16[16,1024]{1,0:T(8,128)(2,1)S(1)}, u32[]{:S(2)}, u32[]{:S(2)}) collective-permute-start(bf16[16,1024]{1,0:T(8,128)(2,1)S(1)} %slice.8), channel_id=1, source_target_pairs={{0,1},{1,2},{2,3},{3,4},{4,5},{5,6},{6,7},{7,8},{8,9},{9,10},{10,1... | collective-permute-start | bytes 98312 | tf_op jit(solution)/shard_map/ppermute | solution.py:279
  103.2 0.7 collective-permute-done.1.refs_1_
  103.8 0.1 broadcast_in_dim.41.refs_9_
  103.9 0.1 broadcast_in_dim.42.refs_10_
  104.0 31.8 %first_merge.1 = (bf16[1024,1024]{1,0:T(8,128)(2,1)S(1)}, bf16[1024,2048]{1,0:T(8,128)(2,1)}, bf16[1024,512]{1,0:T(8,128)(2,1)S(1)}, f32[4,96,256]{2,1,0:T(8,128...) custom-call(bf16[1024,1024]{1,0:T(8,128)(2,1)} %copy-done.2, ...), custom_call_target="tpu_custom_call" | custom-call | tf_op jit(solution)/shard_map/first_merge/pallas_call | solution.py:338
  135.8 1.0 copy-done.6
  136.8 37.2 %all_to_all.20.ext_ref = bf16[32,8,2176]{2,1,0:T(8,128)(2,1)S(1)} all-to-all(bf16[32,8,2176]{2,1,0:T(8,128)(2,1)S(1)} %bitcast.11), channel_id=1, replica_groups=mesh['seq'=32,'head'=1] {'seq'}, dimensions={0} | all-to-all | bytes 2228224 | tf_op jit(solution)/shard_map/all_to_all | solution.py:357
  174.0 1.6 prefix.3
  175.6 2.9 %all-to-all-start.3 = ((bf16[32,8,2048]{2,1,0:T(8,128)(2,1)}), bf16[32,8,2048]{2,1,0:T(8,128)(2,1)S(1)}, u32[]{:S(2)}, u32[]{:S(2)}) async-start(bf16[32,8,2048]{2,1,0:T(8,128)(2,1)} %prefix.3), calls=%async_computation.3 | async-start | bytes 2097152 | tf_op jit(solution)/shard_map/all_to_all | solution.py:409
  178.5 0.0 copy-start.7
  178.5 1.2 copy-done.7
  179.7 18.3 %second.3 = (bf16[1024,2048]{1,0:T(8,128)(2,1)}, bf16[1024,2048]{1,0:T(8,128)(2,1)}) custom-call(bf16[1024,1024]{1,0:T(8,128)(2,1)S(1)} %get-tuple-element.37.refs_0_.stream_ref, f32[1,1024]{1,0:T(1,128)S(1)} %bitcast.19, bf16[1024,2048]{1,0:T(8,128)(2,1)} %refs_2_.7, bf16[1024,2048]{1,0:T(8,128)(2,1)} %get-tuple-element.38.refs_3_, ...), custom_call_target="tpu_custom_call" | custom-call | flops 9797894144 | bytes 25165824 | tf_op jit(solution)/shard_map/second/pallas_call | solution.py:370
  197.9 6.5 %all-to-all-done.3 = bf16[32,8,2048]{2,1,0:T(8,128)(2,1)S(1)} async-done(((bf16[32,8,2048]{2,1,0:T(8,128)(2,1)}), bf16[32,8,2048]{2,1,0:T(8,128)(2,1)S(1)}, u32[]{:S(2)}, u32[]{:S(2)}) %all-to-all-start.3) | async-done | bytes 1048608 | tf_op jit(solution)/shard_map/all_to_all | solution.py:409
  204.5 1.2 copy-done.8
  205.7 13.9 %third.1 = bf16[1024,1024]{1,0:T(8,128)(2,1)} custom-call(bf16[1024,1024]{1,0:T(8,128)(2,1)S(1)} %get-tuple-element.37.refs_0_.stream_ref, bf16[1024,2048]{1,0:T(8,128)(2,1)} %get-tuple-element.42.sg_ref, bf16[1024,2048]{1,0:T(8,128)(2,1)} %get-tuple-element.43.mixed_ref, bf16[1024,512]{1,0:T(8,128)(2,1)S(1)} %copy-done.8, ...), custom_call_target="tpu_custom_call" | custom-call | tf_op jit(solution)/shard_map/third/pallas_call | solution.py:423
  (30 shorter events, 0.1 us)
Async XLA Ops:
  0.7 3.2 %collective-permute-start = (bf16[16,256]{1,0:T(8,128)(2,1)S(1)}, bf16[16,256]{1,0:T(8,128)(2,1)S(1)}, u32[]{:S(2)}, u32[]{:S(2)}) collective-permute-start(bf16[16,256]{1,0:T(8,128)(2,1)S(1)} %slice.6), channel_id=1, source_target_pairs={{0,1},{1,2},{2,3},{3,4},{4,5},{5,6},{6,7},{7,8},{8,9},{9,10},{10,1... | collective-permute-start | bytes 24584 | tf_op jit(solution)/shard_map/ppermute | solution.py:279
  5.3 1.6 copy-start
  6.9 0.9 copy-start.10
  7.9 0.9 copy-start.11
  8.8 0.7 copy-start.14
  9.5 0.7 copy-start.17
  10.2 0.7 copy-start.18
  10.9 0.7 copy-start.22
  11.6 43.1 %copy-start.1 = (bf16[4096,256]{1,0:T(8,128)(2,1)S(1)}, bf16[4096,256]{1,0:T(8,128)(2,1)}, u32[]{:S(2)}) copy-start(bf16[4096,256]{1,0:T(8,128)(2,1)} %stream_ref.1) | copy-start | bytes 6291460
  45.6 21.5 %all-to-all-start = ((bf16[32,8,640]{2,1,0:T(8,128)(2,1)}), bf16[32,8,640]{2,1,0:T(8,128)(2,1)S(1)}, u32[]{:S(2)}, u32[]{:S(2)}) async-start(bf16[32,8,640]{2,1,0:T(8,128)(2,1)} %bitcast.2), calls=%async_computation | async-start | bytes 655360 | tf_op jit(solution)/shard_map/all_to_all | solution.py:357
  54.7 1.0 copy-start.3
  55.7 0.7 copy-start.15
  56.3 17.6 %copy-start.4 = (bf16[256,512]{1,0:T(8,128)(2,1)S(1)}, bf16[256,512]{1,0:T(8,128)(2,1)}, u32[]{:S(2)}) copy-start(bf16[256,512]{1,0:T(8,128)(2,1)} %refs_4_.4) | copy-start | bytes 786436
  56.3 17.6 %copy-start.16 = (f32[256]{0:T(256)S(1)}, f32[256]{0:T(256)}, u32[]{:S(2)}) copy-start(f32[256]{0:T(256)} %param.25) | copy-start | bytes 3076
  68.1 16.6 %all-to-all-start.1 = ((bf16[32,8,512]{2,1,0:T(8,128)(2,1)}), bf16[32,8,512]{2,1,0:T(8,128)(2,1)S(1)}, u32[]{:S(2)}, u32[]{:S(2)}) async-start(bf16[32,8,512]{2,1,0:T(8,128)(2,1)} %prefix.2), calls=%async_computation.1 | async-start | bytes 524288 | tf_op jit(solution)/shard_map/all_to_all | solution.py:409
  74.0 10.8 %copy-start.9 = (bf16[512,256]{1,0:T(8,128)(2,1)S(1)}, bf16[512,256]{1,0:T(8,128)(2,1)}, u32[]{:S(2)}) copy-start(bf16[512,256]{1,0:T(8,128)(2,1)} %output_ref.2) | copy-start | bytes 786436
  74.0 10.8 %copy-start.23 = (f32[512]{0:T(512)S(1)}, f32[512]{0:T(512)}, u32[]{:S(2)}) copy-start(f32[512]{0:T(512)} %param.34) | copy-start | bytes 6148
  84.8 19.1 %copy-start.24 = (f32[32]{0:T(128)S(1)}, f32[32]{0:T(128)}, u32[]{:S(2)}) copy-start(f32[32]{0:T(128)} %param.44) | copy-start | bytes 388
  84.8 19.1 %copy-start.25 = (f32[32]{0:T(128)S(1)}, f32[32]{0:T(128)}, u32[]{:S(2)}) copy-start(f32[32]{0:T(128)} %param.45) | copy-start | bytes 388
  84.8 19.2 %copy-start.5 = (bf16[1024,512]{1,0:T(8,128)(2,1)S(1)}, bf16[1024,512]{1,0:T(8,128)(2,1)}, u32[]{:S(2)}) copy-start(bf16[1024,512]{1,0:T(8,128)(2,1)} %refs_5_.1) | copy-start | bytes 3145732
  84.8 19.2 %copy-start.12 = (bf16[1024,32]{0,1:T(8,128)(2,1)S(1)}, bf16[1024,32]{0,1:T(8,128)(2,1)}, u32[]{:S(2)}) copy-start(bf16[1024,32]{0,1:T(8,128)(2,1)} %param.41) | copy-start | bytes 196612
  84.8 19.2 %copy-start.13 = (f32[4,2048]{1,0:T(4,128)S(1)}, f32[4,2048]{1,0:T(4,128)}, u32[]{:S(2)}) copy-start(f32[4,2048]{1,0:T(4,128)} %refs_7_.3) | copy-start | bytes 98308
  84.8 19.2 %copy-start.19 = (f32[4,512]{1,0:T(4,128)S(1)}, f32[4,512]{1,0:T(4,128)}, u32[]{:S(2)}) copy-start(f32[4,512]{1,0:T(4,128)} %refs_8_.1) | copy-start | bytes 24580
  84.9 19.2 %copy-start.21 = (f32[1024]{0:T(1024)S(1)}, f32[1024]{0:T(1024)}, u32[]{:S(2)}) copy-start(f32[1024]{0:T(1024)} %param.37) | copy-start | bytes 12292
  100.8 3.2 %copy-start.2 = (bf16[1024,1024]{1,0:T(8,128)(2,1)}, bf16[1024,1024]{1,0:T(8,128)(2,1)S(1)}, u32[]{:S(2)}) copy-start(bf16[1024,1024]{1,0:T(8,128)(2,1)S(1)} %third_tiles.1.refs_0_) | copy-start | bytes 6291460
  100.8 3.0 %collective-permute-start.1 = (bf16[16,1024]{1,0:T(8,128)(2,1)S(1)}, bf16[16,1024]{1,0:T(8,128)(2,1)S(1)}, u32[]{:S(2)}, u32[]{:S(2)}) collective-permute-start(bf16[16,1024]{1,0:T(8,128)(2,1)S(1)} %slice.8), channel_id=1, source_target_pairs={{0,1},{1,2},{2,3},{3,4},{4,5},{5,6},{6,7},{7,8},{8,9},{9,10},{10,1... | collective-permute-start | bytes 98312 | tf_op jit(solution)/shard_map/ppermute | solution.py:279
  135.8 1.0 copy-start.6
  175.6 28.9 %all-to-all-start.3 = ((bf16[32,8,2048]{2,1,0:T(8,128)(2,1)}), bf16[32,8,2048]{2,1,0:T(8,128)(2,1)S(1)}, u32[]{:S(2)}, u32[]{:S(2)}) async-start(bf16[32,8,2048]{2,1,0:T(8,128)(2,1)} %prefix.3), calls=%async_computation.3 | async-start | bytes 2097152 | tf_op jit(solution)/shard_map/all_to_all | solution.py:409
  178.5 1.2 copy-start.7
  179.7 24.8 %copy-start.20 = (f32[2048]{0:T(1024)S(1)}, f32[2048]{0:T(1024)}, u32[]{:S(2)}) copy-start(f32[2048]{0:T(1024)} %param.46) | copy-start | bytes 24580
  204.5 1.2 copy-start.8
